TPU v7x, 512 devices: a whole 4x4x16 slice. The times are simulated.
512 devices in a mesh: head: 8 (over z_lo), outer: 8 (over y, z_hi), inner: 8 (over x, core).
Axes of the slice: x: 4, y: 4, z: 16 (z_hi: 2, z_lo: 8; z = z_hi * 8 + z_lo), core: 2. Of those that a mesh axis runs over, the one named last changes fastest.
Arguments:
- query_states: bfloat16 [8, 4096, 4096], P('head', ('outer', 'inner')), may hold values from -24 to 24
- key_states: bfloat16 [8, 4096, 4096], P('head', ('outer', 'inner')), may hold values from -24 to 24
- value_states: bfloat16 [8, 4096, 4096], P('head', ('outer', 'inner')), may hold values from -6 to 6
- output_grad: bfloat16 [8, 4096, 4096], P('head', ('outer', 'inner')), may hold values from -1.5 to 1.5
- saved_offset: float32 [8, 4096, 32], P(None, ('outer', 'inner'), 'head'), may hold values from -6 to 6
- rest_mass: float32 [8, 4096, 32], P(None, ('outer', 'inner'), 'head'), may hold values from 0 to 16
Outputs:
- query_grad: bfloat16 [8, 4096, 4096], P(None, ('outer', 'inner'), 'head')
- key_grad: float32 [8, 4096, 4096], P(None, ('outer', 'inner'), 'head')
- value_grad: float32 [8, 4096, 4096], P(None, ('outer', 'inner'), 'head')
All inputs are finite; a program needn't handle non-finite values.
Results may differ from a plain program's by a relative error of at most 0.012.
Values may be sent and summed in bfloat16 or wider, within the bound.
A program may use at most 128 MiB of HBM per device.

v0:
```python
import jax
import jax.numpy as jnp
from jax import lax
from jax.sharding import PartitionSpec as P


def from_behind(x, axis, by):
    peers = lax.axis_size(axis)
    return lax.ppermute(x, axis, [(i, (i + by) % peers) for i in range(peers)])


def tile_scores(query_tile, key_tile, score_scale):
    return (
        jnp.einsum("qhd,khd->hqk", query_tile, key_tile, preferred_element_type=jnp.float32)
        * score_scale
    )


def fold_stats(row_max, row_sum, scores):
    new_max = jnp.maximum(row_max, jnp.max(scores, axis=-1))
    row_sum = row_sum * jnp.exp(row_max - new_max) + jnp.sum(
        jnp.exp(scores - new_max[:, :, None]), axis=-1
    )
    return (new_max, row_sum)


def combine_norm(row_max, row_sum, rest_local):
    ceiling = jnp.maximum(row_max, rest_local)
    return ceiling + jnp.log(row_sum * jnp.exp(row_max - ceiling) + jnp.exp(rest_local - ceiling))


def tile_grads(query_tile, grad_tile, key_tile, value_tile, log_norm, offset, score_scale):
    scores = tile_scores(query_tile, key_tile, score_scale)
    weights = jnp.exp(scores - log_norm[:, :, None])
    weights_low = weights.astype(jnp.bfloat16)
    dweights = jnp.einsum("qhd,khd->hqk", grad_tile, value_tile, preferred_element_type=jnp.float32)
    dscores = (weights * (dweights - offset[:, :, None])).astype(jnp.bfloat16)
    query_term = (
        jnp.einsum("hqk,khd->qhd", dscores, key_tile, preferred_element_type=jnp.float32)
        * score_scale
    )
    key_term = (
        jnp.einsum("hqk,qhd->khd", dscores, query_tile, preferred_element_type=jnp.float32)
        * score_scale
    )
    value_term = jnp.einsum(
        "hqk,qhd->khd", weights_low, grad_tile, preferred_element_type=jnp.float32
    )
    return (query_term, key_term, value_term)


def body(query_states, key_states, value_states, output_grad, saved_offset, rest_mass):
    pieces = (
        lax.all_to_all(query_states, "head", split_axis=2, concat_axis=0, tiled=True),
        lax.all_to_all(key_states, "head", split_axis=2, concat_axis=0, tiled=True),
        lax.all_to_all(value_states, "head", split_axis=2, concat_axis=0, tiled=True),
        lax.all_to_all(output_grad, "head", split_axis=2, concat_axis=0, tiled=True),
    )
    groups, group_tokens, lane_width = pieces[0].shape
    block_rows = groups * group_tokens
    head_count = rest_mass.shape[2]
    head_size = lane_width // head_count
    score_scale = float(head_size) ** (-0.5)
    query_tile, key_tile, value_tile, grad_tile = [
        arrived.reshape(block_rows, head_count, head_size) for arrived in pieces
    ]
    rest_local = rest_mass.reshape(block_rows, head_count).T
    offset = saved_offset.reshape(block_rows, head_count).T
    window = lax.axis_size("inner") // 2
    start_max = jnp.full((head_count, block_rows), -jnp.inf, jnp.float32)
    start_sum = jnp.zeros((head_count, block_rows), jnp.float32)
    query_acc = jnp.zeros(query_tile.shape, jnp.float32)
    key_acc = jnp.zeros((block_rows, lane_width), jnp.float32)
    value_acc = jnp.zeros((block_rows, lane_width), jnp.float32)
    row_max, row_sum = (start_max, start_sum)
    key_block = key_tile
    for hop_index in range(window):
        row_max, row_sum = fold_stats(
            row_max, row_sum, tile_scores(query_tile, key_block, score_scale)
        )
        if hop_index + 1 < window:
            key_block = from_behind(key_block, ("outer", "inner"), 1)
    log_norm = combine_norm(row_max, row_sum, rest_local)
    key_block, value_block = (key_tile, value_tile)
    for hop_index in range(window):
        query_term, key_term, value_term = tile_grads(
            query_tile, grad_tile, key_block, value_block, log_norm, offset, score_scale
        )
        query_acc = query_acc + query_term
        key_acc = key_acc + key_term.reshape(block_rows, lane_width)
        value_acc = value_acc + value_term.reshape(block_rows, lane_width)
        if hop_index + 1 < window:
            key_block, value_block = from_behind((key_block, value_block), ("outer", "inner"), 1)
        key_acc, value_acc = (
            from_behind(key_acc.astype(jnp.bfloat16), ("outer", "inner"), 1).astype(key_acc.dtype),
            from_behind(value_acc.astype(jnp.bfloat16), ("outer", "inner"), 1).astype(
                value_acc.dtype
            ),
        )
    return (
        query_acc.reshape(groups, group_tokens, lane_width).astype(jnp.bfloat16),
        key_acc.reshape(groups, group_tokens, lane_width),
        value_acc.reshape(groups, group_tokens, lane_width),
    )


def solution(mesh):
    placed = (
        P("head", ("outer", "inner"), None),
        P("head", ("outer", "inner"), None),
        P("head", ("outer", "inner"), None),
        P("head", ("outer", "inner"), None),
        P(None, ("outer", "inner"), "head"),
        P(None, ("outer", "inner"), "head"),
    )
    return jax.shard_map(
        body,
        mesh=mesh,
        in_specs=placed,
        out_specs=(
            P(None, ("outer", "inner"), "head"),
            P(None, ("outer", "inner"), "head"),
            P(None, ("outer", "inner"), "head"),
        ),
        check_vma=False,
    )
```

profile of v0, /device:TPU:24, one launch (start us, length us, event | category | flops | bytes accessed | tf_op | source)
XLA Modules:
  0.0 544.8 jit_solution(2273492320403466222)
XLA Ops:
  0.6 4.9 copy.207
  6.1 22.4 %reduce.1 = bf16[4096,64]{1,0:T(8,128)(2,1)S(1)} reduce(bf16[4096,1,64]{2,1,0:T(2,128)(2,1)S(1)} %bitcast.165, bf16[]{:T(256)} %broadcast.55), dimensions={1}, to_apply=%bitcast.116.reduce_sub_computation | reduce | bytes 1048578
  30.0 12.8 %all-to-all-start.1 = ((bf16[8,2,16384]{2,1,0:T(2,128)(2,1)}), bf16[8,2,16384]{2,1,0:T(2,128)(2,1)}, u32[]{:S(2)}, u32[]{:S(2)}) async-start(bf16[8,2,16384]{2,1,0:T(2,128)(2,1)} %reshape.110), calls=%async_computation.1 | async-start | bytes 1048576 | tf_op jit(solution)/shard_map/all_to_all | solution.py:55
  42.8 4.9 copy.204
  47.6 22.4 %reduce = bf16[4096,64]{1,0:T(8,128)(2,1)S(1)} reduce(bf16[4096,1,64]{2,1,0:T(2,128)(2,1)S(1)} %bitcast.167, bf16[]{:T(256)} %broadcast.55), dimensions={1}, to_apply=%bitcast.118.reduce_sub_computation | reduce | bytes 1048578
  71.6 10.2 %all-to-all-start = ((bf16[8,2,16384]{2,1,0:T(2,128)(2,1)}), bf16[8,2,16384]{2,1,0:T(2,128)(2,1)}, u32[]{:S(2)}, u32[]{:S(2)}) async-start(bf16[8,2,16384]{2,1,0:T(2,128)(2,1)} %reshape.112), calls=%async_computation | async-start | bytes 1048576 | tf_op jit(solution)/shard_map/all_to_all | solution.py:54
  81.7 4.9 copy.220
  86.6 22.4 %reduce.3 = bf16[4096,64]{1,0:T(8,128)(2,1)S(1)} reduce(bf16[4096,1,64]{2,1,0:T(2,128)(2,1)S(1)} %bitcast.168, bf16[]{:T(256)} %broadcast.55), dimensions={1}, to_apply=%bitcast.120.reduce_sub_computation | reduce | bytes 1048578
  110.5 10.2 %all-to-all-start.3 = ((bf16[8,2,16384]{2,1,0:T(2,128)(2,1)}), bf16[8,2,16384]{2,1,0:T(2,128)(2,1)}, u32[]{:S(2)}, u32[]{:S(2)}) async-start(bf16[8,2,16384]{2,1,0:T(2,128)(2,1)} %reshape.114), calls=%async_computation.3 | async-start | bytes 1048576 | tf_op jit(solution)/shard_map/all_to_all | solution.py:56
  120.7 4.9 copy.217
  125.6 22.4 %reduce.2 = bf16[4096,64]{1,0:T(8,128)(2,1)S(1)} reduce(bf16[4096,1,64]{2,1,0:T(2,128)(2,1)S(1)} %bitcast.166, bf16[]{:T(256)} %broadcast.55), dimensions={1}, to_apply=%bitcast.122.reduce_sub_computation | reduce | bytes 1048578
  149.5 9.9 %all-to-all-start.2 = ((bf16[8,2,16384]{2,1,0:T(2,128)(2,1)}), bf16[8,2,16384]{2,1,0:T(2,128)(2,1)}, u32[]{:S(2)}, u32[]{:S(2)}) async-start(bf16[8,2,16384]{2,1,0:T(2,128)(2,1)} %reshape.116), calls=%async_computation.2 | async-start | bytes 1048576 | tf_op jit(solution)/shard_map/all_to_all | solution.py:57
  159.4 4.1 reshape.111
  163.6 2.3 copy.208
  169.5 4.1 reshape.113
  173.6 2.3 copy.205
  176.1 4.1 reshape.115
  180.2 2.3 copy.221
  184.0 3.5 collective-permute-start.3
  189.2 4.1 reshape.117
  193.4 3.6 copy.218
  198.2 2.4 collective-permute-start.1
  200.6 2.7 multiply_reduce_fusion.3
  203.3 39.4 %collective-permute-done.3 = bf16[512,4,128]{2,0,1:T(8,128)(2,1)} collective-permute-done((bf16[512,4,128]{2,0,1:T(8,128)(2,1)}, bf16[512,4,128]{2,0,1:T(8,128)(2,1)}, u32[]{:S(2)}, u32[]{:S(2)}) %collective-permute-start.3) | collective-permute-done | bytes 524320 | tf_op jit(solution)/shard_map/ppermute | solution.py:9
  246.4 8.7 %collective-permute-done.1 = bf16[512,4,128]{2,0,1:T(8,128)(2,1)S(1)} collective-permute-done((bf16[512,4,128]{2,0,1:T(8,128)(2,1)}, bf16[512,4,128]{2,0,1:T(8,128)(2,1)S(1)}, u32[]{:S(2)}, u32[]{:S(2)}) %collective-permute-start.1) | collective-permute-done | bytes 524320 | tf_op jit(solution)/shard_map/ppermute | solution.py:9
  258.7 36.8 %collective-permute-done.4 = bf16[512,4,128]{2,0,1:T(8,128)(2,1)} collective-permute-done((bf16[512,4,128]{2,0,1:T(8,128)(2,1)}, bf16[512,4,128]{2,0,1:T(8,128)(2,1)}, u32[]{:S(2)}, u32[]{:S(2)}) %collective-permute-start.4) | collective-permute-done | bytes 524320 | tf_op jit(solution)/shard_map/ppermute | solution.py:9
  298.1 73.5 %collective-permute-done.2 = bf16[512,4,128]{2,0,1:T(8,128)(2,1)S(1)} collective-permute-done((bf16[512,4,128]{2,0,1:T(8,128)(2,1)S(1)}, bf16[512,4,128]{2,0,1:T(8,128)(2,1)S(1)}, u32[]{:S(2)}, u32[]{:S(2)}) %collective-permute-start.2) | collective-permute-done | bytes 524320 | tf_op jit(solution)/shard_map/ppermute | solution.py:9
  379.5 2.1 collective-permute-start.10
  382.7 2.5 multiply_convert_fusion.2
  390.1 2.2 collective-permute-start.6
  392.2 3.3 multiply_convert_fusion.1
  399.2 2.1 multiply_convert_fusion
  404.3 2.6 copy.247
  406.9 2.6 copy.251
  409.5 2.5 copy.255
  412.0 3.3 fusion.4
  415.3 7.7 %collective-permute-done.10 = bf16[512,512]{0,1:T(8,128)(2,1)} collective-permute-done((bf16[512,512]{0,1:T(8,128)(2,1)}, bf16[512,512]{0,1:T(8,128)(2,1)}, u32[]{:S(2)}, u32[]{:S(2)}) %collective-permute-start.10) | collective-permute-done | bytes 524320 | tf_op jit(solution)/shard_map/ppermute | solution.py:9
  426.3 2.5 collective-permute-done.6
  430.1 2.1 collective-permute-start.7
  433.1 38.1 %collective-permute-done.11 = bf16[512,512]{0,1:T(8,128)(2,1)S(1)} collective-permute-done((bf16[512,512]{0,1:T(8,128)(2,1)S(1)}, bf16[512,512]{0,1:T(8,128)(2,1)S(1)}, u32[]{:S(2)}, u32[]{:S(2)}) %collective-permute-start.11) | collective-permute-done | bytes 524320 | tf_op jit(solution)/shard_map/ppermute | solution.py:9
  471.4 2.1 collective-permute-start.12
  473.4 3.5 collective-permute-done.7
  481.1 29.6 %collective-permute-done.12 = bf16[512,512]{0,1:T(8,128)(2,1)S(1)} collective-permute-done((bf16[512,512]{0,1:T(8,128)(2,1)S(1)}, bf16[512,512]{0,1:T(8,128)(2,1)S(1)}, u32[]{:S(2)}, u32[]{:S(2)}) %collective-permute-start.12) | collective-permute-done | bytes 524320 | tf_op jit(solution)/shard_map/ppermute | solution.py:9
  511.7 2.1 collective-permute-start.13
  513.8 2.6 collective-permute-done.8
  522.5 14.1 %collective-permute-done.13 = bf16[512,512]{0,1:T(8,128)(2,1)S(1)} collective-permute-done((bf16[512,512]{0,1:T(8,128)(2,1)}, bf16[512,512]{0,1:T(8,128)(2,1)S(1)}, u32[]{:S(2)}, u32[]{:S(2)}) %collective-permute-start.13) | collective-permute-done | bytes 524320 | tf_op jit(solution)/shard_map/ppermute | solution.py:9
  537.8 4.5 collective-permute-done.9
  542.3 2.2 copy.256
  (123 shorter events, 62.9 us)
Async XLA Ops:
  30.0 41.6 %all-to-all-start.1 = ((bf16[8,2,16384]{2,1,0:T(2,128)(2,1)}), bf16[8,2,16384]{2,1,0:T(2,128)(2,1)}, u32[]{:S(2)}, u32[]{:S(2)}) async-start(bf16[8,2,16384]{2,1,0:T(2,128)(2,1)} %reshape.110), calls=%async_computation.1 | async-start | bytes 1048576 | tf_op jit(solution)/shard_map/all_to_all | solution.py:55
  71.6 39.0 %all-to-all-start = ((bf16[8,2,16384]{2,1,0:T(2,128)(2,1)}), bf16[8,2,16384]{2,1,0:T(2,128)(2,1)}, u32[]{:S(2)}, u32[]{:S(2)}) async-start(bf16[8,2,16384]{2,1,0:T(2,128)(2,1)} %reshape.112), calls=%async_computation | async-start | bytes 1048576 | tf_op jit(solution)/shard_map/all_to_all | solution.py:54
  110.5 39.0 %all-to-all-start.3 = ((bf16[8,2,16384]{2,1,0:T(2,128)(2,1)}), bf16[8,2,16384]{2,1,0:T(2,128)(2,1)}, u32[]{:S(2)}, u32[]{:S(2)}) async-start(bf16[8,2,16384]{2,1,0:T(2,128)(2,1)} %reshape.114), calls=%async_computation.3 | async-start | bytes 1048576 | tf_op jit(solution)/shard_map/all_to_all | solution.py:56
  149.5 39.7 %all-to-all-start.2 = ((bf16[8,2,16384]{2,1,0:T(2,128)(2,1)}), bf16[8,2,16384]{2,1,0:T(2,128)(2,1)}, u32[]{:S(2)}, u32[]{:S(2)}) async-start(bf16[8,2,16384]{2,1,0:T(2,128)(2,1)} %reshape.116), calls=%async_computation.2 | async-start | bytes 1048576 | tf_op jit(solution)/shard_map/all_to_all | solution.py:57
  163.6 5.7 %copy-start.25 = (f32[8,64,4]{1,2,0:T(4,128)S(1)}, f32[8,64,4]{1,2,0:T(4,128)}, u32[]{:S(2)}) copy-start(f32[8,64,4]{1,2,0:T(4,128)} %param.11) | copy-start | bytes 24580
  163.6 5.8 %copy-start.26 = (f32[8,64,4]{1,2,0:T(4,128)S(1)}, f32[8,64,4]{1,2,0:T(4,128)}, u32[]{:S(2)}) copy-start(f32[8,64,4]{1,2,0:T(4,128)} %param.10) | copy-start | bytes 24580
  166.4 3.0 copy-start.11
  167.4 30.8 %collective-permute-start = (bf16[512,4,128]{2,0,1:T(8,128)(2,1)}, bf16[512,4,128]{2,0,1:T(8,128)(2,1)}, u32[]{:S(2)}, u32[]{:S(2)}) collective-permute-start(bf16[512,4,128]{2,0,1:T(8,128)(2,1)} %copy.211), channel_id=1, source_target_pairs={{0,1},{1,2},{2,3},{3,4},{4,5},{5,6},{6,7},{7,8},{8,9},{9,10},{10,1... | collective-permute-start | bytes 1572872 | tf_op jit(solution)/shard_map/ppermute | solution.py:9
  183.0 4.5 copy-start.14
  184.0 58.7 %collective-permute-start.3 = (bf16[512,4,128]{2,0,1:T(8,128)(2,1)}, bf16[512,4,128]{2,0,1:T(8,128)(2,1)}, u32[]{:S(2)}, u32[]{:S(2)}) collective-permute-start(bf16[512,4,128]{2,0,1:T(8,128)(2,1)} %copy.224), channel_id=1, source_target_pairs={{0,1},{1,2},{2,3},{3,4},{4,5},{5,6},{6,7},{7,8},{8,9},{9,10},{10,1... | collective-permute-start | bytes 1572872 | tf_op jit(solution)/shard_map/ppermute | solution.py:9
  188.6 12.0 %copy-start.12 = (bf16[512,4,128]{2,1,0:T(4,128)(2,1)S(1)}, bf16[512,4,128]{2,1,0:T(4,128)(2,1)}, u32[]{:S(2)}) copy-start(bf16[512,4,128]{2,1,0:T(4,128)(2,1)} %copy-done.11) | copy-start | bytes 1572868
  198.2 56.8 %collective-permute-start.1 = (bf16[512,4,128]{2,0,1:T(8,128)(2,1)}, bf16[512,4,128]{2,0,1:T(8,128)(2,1)S(1)}, u32[]{:S(2)}, u32[]{:S(2)}) collective-permute-start(bf16[512,4,128]{2,0,1:T(8,128)(2,1)} %collective-permute-done), channel_id=1, source_target_pairs={{0,1},{1,2},{2,3},{3,4},{4,5},{5,6},{6,7},{7,8},{8,9},{9,10},{10,1... | collective-permute-start | bytes 1572872 | tf_op jit(solution)/shard_map/ppermute | solution.py:9
  242.7 52.8 %collective-permute-start.4 = (bf16[512,4,128]{2,0,1:T(8,128)(2,1)}, bf16[512,4,128]{2,0,1:T(8,128)(2,1)}, u32[]{:S(2)}, u32[]{:S(2)}) collective-permute-start(bf16[512,4,128]{2,0,1:T(8,128)(2,1)} %collective-permute-done.3), channel_id=1, source_target_pairs={{0,1},{1,2},{2,3},{3,4},{4,5},{5,6},{6,7},{7,8},{8,9},{9,10},{10,1... | collective-permute-start | bytes 1572872 | tf_op jit(solution)/shard_map/ppermute | solution.py:9
  255.0 43.1 %copy-start.21 = (bf16[512,4,128]{2,0,1:T(8,128)(2,1)}, bf16[512,4,128]{2,0,1:T(8,128)(2,1)S(1)}, u32[]{:S(2)}) copy-start(bf16[512,4,128]{2,0,1:T(8,128)(2,1)S(1)} %collective-permute-done.1) | copy-start | bytes 1572868
  255.0 116.6 %collective-permute-start.2 = (bf16[512,4,128]{2,0,1:T(8,128)(2,1)S(1)}, bf16[512,4,128]{2,0,1:T(8,128)(2,1)S(1)}, u32[]{:S(2)}, u32[]{:S(2)}) collective-permute-start(bf16[512,4,128]{2,0,1:T(8,128)(2,1)S(1)} %collective-permute-done.1), channel_id=1, source_target_pairs={{0,1},{1,2},{2,3},{3,4},{4,5},{5,6},{6,7},{7,8},{8,9},{9,10},{10,1... | collective-permute-start | bytes 1572872 | tf_op jit(solution)/shard_map/ppermute | solution.py:9
  258.7 113.7 %copy-start = (f32[4,512,512]{1,2,0:T(8,128)S(1)}, f32[4,512,512]{1,2,0:T(8,128)}, u32[]{:S(2)}) copy-start(f32[4,512,512]{1,2,0:T(8,128)} %get-tuple-element.14) | copy-start | bytes 12582916
  295.5 103.7 %collective-permute-start.5 = (bf16[512,4,128]{2,0,1:T(8,128)(2,1)}, bf16[512,4,128]{2,0,1:T(8,128)(2,1)}, u32[]{:S(2)}, u32[]{:S(2)}) collective-permute-start(bf16[512,4,128]{2,0,1:T(8,128)(2,1)} %collective-permute-done.4), channel_id=1, source_target_pairs={{0,1},{1,2},{2,3},{3,4},{4,5},{5,6},{6,7},{7,8},{8,9},{9,10},{10,1... | collective-permute-start | bytes 1572872 | tf_op jit(solution)/shard_map/ppermute | solution.py:9
  298.1 75.7 %copy-start.3 = (f32[4,512,512]{1,2,0:T(8,128)}, f32[4,512,512]{1,2,0:T(8,128)S(1)}, u32[]{:S(2)}) copy-start(f32[4,512,512]{1,2,0:T(8,128)S(1)} %get-tuple-element.12) | copy-start | bytes 12582916
  371.6 2.2 copy-start.23
  372.3 1.9 copy-start.1
  375.7 5.8 %copy-start.15 = (bf16[512,4,128]{2,1,0:T(4,128)(2,1)S(1)}, bf16[512,4,128]{2,1,0:T(4,128)(2,1)}, u32[]{:S(2)}) copy-start(bf16[512,4,128]{2,1,0:T(4,128)(2,1)} %copy-done.14) | copy-start | bytes 1572868
  379.5 43.5 %collective-permute-start.10 = (bf16[512,512]{0,1:T(8,128)(2,1)}, bf16[512,512]{0,1:T(8,128)(2,1)}, u32[]{:S(2)}, u32[]{:S(2)}) collective-permute-start(bf16[512,512]{0,1:T(8,128)(2,1)} %bitcast.17), channel_id=1, source_target_pairs={{0,1},{1,2},{2,3},{3,4},{4,5},{5,6},{6,7},{7,8},{8,9},{9,10},{10,1... | collective-permute-start | bytes 1572872 | tf_op jit(solution)/shard_map/ppermute | solution.py:9
  382.7 5.6 %copy-start.9 = (bf16[4,512,512]{1,2,0:T(8,128)(2,1)}, bf16[4,512,512]{1,2,0:T(8,128)(2,1)S(1)}, u32[]{:S(2)}) copy-start(bf16[4,512,512]{1,2,0:T(8,128)(2,1)S(1)} %multiply_convert_fusion.3) | copy-start | bytes 6291460
  385.2 1.4 copy-start.7
  390.0 7.2 %copy-start.4 = (f32[4,512,512]{1,2,0:T(8,128)S(1)}, f32[4,512,512]{1,2,0:T(8,128)}, u32[]{:S(2)}) copy-start(f32[4,512,512]{1,2,0:T(8,128)} %copy-done.3) | copy-start | bytes 12582916
  390.1 38.8 %collective-permute-start.6 = (bf16[512,512]{0,1:T(8,128)(2,1)}, bf16[512,512]{0,1:T(8,128)(2,1)}, u32[]{:S(2)}, u32[]{:S(2)}) collective-permute-start(bf16[512,512]{0,1:T(8,128)(2,1)} %bitcast.8), channel_id=1, source_target_pairs={{0,1},{1,2},{2,3},{3,4},{4,5},{5,6},{6,7},{7,8},{8,9},{9,10},{10,1... | collective-permute-start | bytes 1572872 | tf_op jit(solution)/shard_map/ppermute | solution.py:9
  395.6 3.6 copy-start.2
  401.3 1.4 copy-start.5
  412.0 11.0 %copy-start.20 = (f32[4,512,128]{1,2,0:T(8,128)S(1)}, f32[4,512,128]{1,2,0:T(8,128)}, u32[]{:S(2)}) copy-start(f32[4,512,128]{1,2,0:T(8,128)} %fusion.8) | copy-start | bytes 3145732
  412.0 16.8 %copy-start.18 = (f32[512,4,128]{0,2,1:T(8,128)S(1)}, f32[512,4,128]{0,2,1:T(8,128)}, u32[]{:S(2)}) copy-start(f32[512,4,128]{0,2,1:T(8,128)} %copy.247) | copy-start | bytes 3145732
  412.0 20.1 %copy-start.10 = (bf16[4,512,512]{1,2,0:T(8,128)(2,1)S(1)}, bf16[4,512,512]{1,2,0:T(8,128)(2,1)}, u32[]{:S(2)}) copy-start(bf16[4,512,512]{1,2,0:T(8,128)(2,1)} %copy-done.9) | copy-start | bytes 6291460
  412.0 20.1 %copy-start.13 = (bf16[512,4,128]{2,1,0:T(4,128)(2,1)S(1)}, bf16[512,4,128]{2,1,0:T(4,128)(2,1)}, u32[]{:S(2)}) copy-start(bf16[512,4,128]{2,1,0:T(4,128)(2,1)} %copy-done.11) | copy-start | bytes 1572868
  415.3 55.9 %copy-start.19 = (f32[4,512,128]{1,2,0:T(8,128)S(1)}, f32[4,512,128]{1,2,0:T(8,128)}, u32[]{:S(2)}) copy-start(f32[4,512,128]{1,2,0:T(8,128)} %fusion.6) | copy-start | bytes 3145732
  424.2 52.7 %copy-start.17 = (f32[512,4,128]{0,2,1:T(8,128)S(1)}, f32[512,4,128]{0,2,1:T(8,128)}, u32[]{:S(2)}) copy-start(f32[512,4,128]{0,2,1:T(8,128)} %copy.251) | copy-start | bytes 3145732
  424.3 46.9 %collective-permute-start.11 = (bf16[512,512]{0,1:T(8,128)(2,1)S(1)}, bf16[512,512]{0,1:T(8,128)(2,1)S(1)}, u32[]{:S(2)}, u32[]{:S(2)}) collective-permute-start(bf16[512,512]{0,1:T(8,128)(2,1)S(1)} %fusion.33), channel_id=1, source_target_pairs={{0,1},{1,2},{2,3},{3,4},{4,5},{5,6},{6,7},{7,8},{8,9},{9,10},{10,1... | collective-permute-start | bytes 1572872 | tf_op jit(solution)/shard_map/ppermute | solution.py:9
  430.1 49.1 %copy-start.8 = (bf16[4,512,512]{1,2,0:T(8,128)(2,1)S(1)}, bf16[4,512,512]{1,2,0:T(8,128)(2,1)}, u32[]{:S(2)}) copy-start(bf16[4,512,512]{1,2,0:T(8,128)(2,1)} %copy-done.7) | copy-start | bytes 6291460
  430.1 46.8 %collective-permute-start.7 = (bf16[512,512]{0,1:T(8,128)(2,1)S(1)}, bf16[512,512]{0,1:T(8,128)(2,1)S(1)}, u32[]{:S(2)}, u32[]{:S(2)}) collective-permute-start(bf16[512,512]{0,1:T(8,128)(2,1)S(1)} %fusion.36), channel_id=1, source_target_pairs={{0,1},{1,2},{2,3},{3,4},{4,5},{5,6},{6,7},{7,8},{8,9},{9,10},{10,1... | collective-permute-start | bytes 1572872 | tf_op jit(solution)/shard_map/ppermute | solution.py:9
  471.4 45.1 %copy-start.16 = (f32[512,4,128]{0,2,1:T(8,128)S(1)}, f32[512,4,128]{0,2,1:T(8,128)}, u32[]{:S(2)}) copy-start(f32[512,4,128]{0,2,1:T(8,128)} %copy.255) | copy-start | bytes 3145732
  471.4 39.3 %collective-permute-start.12 = (bf16[512,512]{0,1:T(8,128)(2,1)S(1)}, bf16[512,512]{0,1:T(8,128)(2,1)S(1)}, u32[]{:S(2)}, u32[]{:S(2)}) collective-permute-start(bf16[512,512]{0,1:T(8,128)(2,1)S(1)} %fusion.32), channel_id=1, source_target_pairs={{0,1},{1,2},{2,3},{3,4},{4,5},{5,6},{6,7},{7,8},{8,9},{9,10},{10,1... | collective-permute-start | bytes 1572872 | tf_op jit(solution)/shard_map/ppermute | solution.py:9
  477.1 42.2 %copy-start.22 = (bf16[512,4,128]{2,0,1:T(8,128)(2,1)S(1)}, bf16[512,4,128]{2,0,1:T(8,128)(2,1)}, u32[]{:S(2)}) copy-start(bf16[512,4,128]{2,0,1:T(8,128)(2,1)} %copy-done.21) | copy-start | bytes 1572868
  477.1 39.3 %collective-permute-start.8 = (bf16[512,512]{0,1:T(8,128)(2,1)S(1)}, bf16[512,512]{0,1:T(8,128)(2,1)S(1)}, u32[]{:S(2)}, u32[]{:S(2)}) collective-permute-start(bf16[512,512]{0,1:T(8,128)(2,1)S(1)} %fusion.35), channel_id=1, source_target_pairs={{0,1},{1,2},{2,3},{3,4},{4,5},{5,6},{6,7},{7,8},{8,9},{9,10},{10,1... | collective-permute-start | bytes 1572872 | tf_op jit(solution)/shard_map/ppermute | solution.py:9
  481.1 39.1 %copy-start.6 = (bf16[4,512,512]{1,2,0:T(8,128)(2,1)S(1)}, bf16[4,512,512]{1,2,0:T(8,128)(2,1)}, u32[]{:S(2)}) copy-start(bf16[4,512,512]{1,2,0:T(8,128)(2,1)} %copy-done.5) | copy-start | bytes 6291460
  481.1 39.1 %copy-start.24 = (bf16[512,4,128]{2,0,1:T(8,128)(2,1)S(1)}, bf16[512,4,128]{2,0,1:T(8,128)(2,1)}, u32[]{:S(2)}) copy-start(bf16[512,4,128]{2,0,1:T(8,128)(2,1)} %copy-done.23) | copy-start | bytes 1572868
  511.7 24.9 %collective-permute-start.13 = (bf16[512,512]{0,1:T(8,128)(2,1)}, bf16[512,512]{0,1:T(8,128)(2,1)S(1)}, u32[]{:S(2)}, u32[]{:S(2)}) collective-permute-start(bf16[512,512]{0,1:T(8,128)(2,1)} %fusion.31), channel_id=1, source_target_pairs={{0,1},{1,2},{2,3},{3,4},{4,5},{5,6},{6,7},{7,8},{8,9},{9,10},{10,1... | collective-permute-start | bytes 1572872 | tf_op jit(solution)/shard_map/ppermute | solution.py:9
  517.4 24.9 %collective-permute-start.9 = (bf16[512,512]{0,1:T(8,128)(2,1)}, bf16[512,512]{0,1:T(8,128)(2,1)}, u32[]{:S(2)}, u32[]{:S(2)}) collective-permute-start(bf16[512,512]{0,1:T(8,128)(2,1)} %fusion.34), channel_id=1, source_target_pairs={{0,1},{1,2},{2,3},{3,4},{4,5},{5,6},{6,7},{7,8},{8,9},{9,10},{10,1... | collective-permute-start | bytes 1572872 | tf_op jit(solution)/shard_map/ppermute | solution.py:9
where the time goes:
time: 553 us; the launch traced here: 545 us
  waiting for transfers between devices  261 us (47%)
  other arithmetic  97.3 us (18%)
  local copies, waits for them, and re-layouts  77.7 us (14%)
  starting transfers between devices  73.1 us (13%)
  matrix products  34.1 us (6%)
    ppermute x14, waiting for transfers between devices, from_behind(): return lax.ppermute(x, axis, [(i, (i + by) % peers) for i in range(peers)])  261 us
    unnamed x4, other arithmetic  89.6 us
    unnamed x73, local copies, waits for them, and re-layouts  47.7 us
    ppermute x14, starting transfers between devices, from_behind(): return lax.ppermute(x, axis, [(i, (i + by) % peers) for i in range(peers)])  30 us
    all_to_all x1, starting transfers between devices, body(): lax.all_to_all(key_states, 'head', split_axis=2, concat_axis=0, tiled=True)  12.8 us
  transfers between devices with their start and end apart: 18, of which 12 were waited for; matrix products, arithmetic and copies ran while one was open for 32% of the time, Pallas kernels for 0%

commit v1 on v0

v1 whole, which is shorter than its diff:
```python
import functools
import math

import jax
import jax.numpy as jnp
from jax import lax
from jax.experimental import pallas as pl
from jax.experimental.pallas import tpu as pltpu
from jax.sharding import PartitionSpec as P

MESH = pl.DeviceIdType.MESH
F32 = jnp.float32
BF16 = jnp.bfloat16

KEY, VALUE, QUERY, GRAD = range(4)
WINDOW = 4
PEER_ORDER = (4, 3, 5, 2, 6, 1, 7)
BORDER_SLOT = {7: 1, 6: 2, 5: 3, 4: 4}
BORDER_SENDER = {7: 7, 6: 0, 5: 3, 4: 4}
LEAD = 1


def nt(a, b):
    return lax.dot_general(a, b, (((1,), (1,)), ((), ())), preferred_element_type=F32)


def nn(a, b):
    return lax.dot_general(a, b, (((1,), (0,)), ((), ())), preferred_element_type=F32)


def tn(a, b):
    return lax.dot_general(a, b, (((0,), (0,)), ((), ())), preferred_element_type=F32)


def kernel(
    keys, values, queries, grads, stats_in, query_out, key_out, value_out,
    blk, hop, aux, weights, dscores, key_acc, value_acc, row_factor,
    home_send, home_recv, own_sem, ring_send, ring_recv, hop_send, hop_recv,
    border_send, aux_send, aux_recv,
):
    h, o, i = lax.axis_index("head"), lax.axis_index("outer"), lax.axis_index("inner")
    arrays = (keys, values, queries, grads)
    heads = 4
    rows, size = 64, 128
    block = 8 * rows
    scale = float(size) ** -0.5
    scale2 = scale * math.log2(math.e)
    next_o, last_o = lax.rem(o + 1, 8), lax.rem(o + 7, 8)
    my_rows = pl.ds(pl.multiple_of(h * rows, rows), rows)

    def ahead(by):
        at = i + by
        return (h, jnp.where(at > 7, next_o, o), lax.rem(at, 8))

    def behind(by):
        at = i + 8 - by
        return (h, jnp.where(at < 8, last_o, o), lax.rem(at, 8))

    barrier = pltpu.get_barrier_semaphore()

    def greet(device):
        pl.semaphore_signal(barrier, inc=1, device_id=device, device_id_type=MESH)

    for d in range(1, 8):
        greet((lax.rem(h + d, 8), o, i))
    for d in range(1, WINDOW + 1):
        greet(behind(d))

    @pl.when(i == 3)
    def _():
        greet((h, o, 5))

    @pl.when(i == 0)
    def _():
        greet((h, o, 6))
        for d in range(8):
            for sender in BORDER_SENDER.values():
                greet((lax.rem(h + d, 8), last_o, sender))

    sends_border = (i == 0) | (i == 3) | (i == 4) | (i == 7)
    sends_hop = (i == 5) | (i == 6)
    relays = (i == 0) | (i == 3)

    for a in range(4):
        for j in range(heads):
            pltpu.make_async_copy(
                arrays[a].at[0, :, pl.ds(pl.multiple_of(h * 512 + j * size, size), size)],
                blk.at[0, a, j, my_rows, :],
                own_sem,
            ).start()

    pl.semaphore_wait(
        barrier, 7 + WINDOW + jnp.where(sends_border, 8, 0) + jnp.where(sends_hop, 1, 0)
    )

    def columns(t, j):
        return pl.ds(pl.multiple_of(t * 512 + j * size, size), size)

    def hop_copy(j, a, t):
        return pltpu.make_async_remote_copy(
            src_ref=arrays[a].at[0, :, columns(t, j)],
            dst_ref=hop.at[a, j, t],
            send_sem=hop_send,
            recv_sem=hop_recv.at[j, a],
            device_id=(h, o, jnp.where(i == 5, 3, 0)),
            device_id_type=MESH,
        )

    def border_copy(j, a, t, slot, source):
        return pltpu.make_async_remote_copy(
            src_ref=source,
            dst_ref=blk.at[slot, a, j, my_rows, :],
            send_sem=border_send,
            recv_sem=ring_recv.at[slot - 1, j, a],
            device_id=(t, next_o, 0),
            device_id_type=MESH,
        )

    def send_hops(j):
        for a in range(4):
            for t in range(8):
                hop_copy(j, a, t).start()

    def send_unit(j, a):
        for d in PEER_ORDER:
            t = lax.rem(h + d, 8)
            pltpu.make_async_remote_copy(
                src_ref=arrays[a].at[0, :, columns(t, j)],
                dst_ref=blk.at[0, a, j, my_rows, :],
                send_sem=home_send,
                recv_sem=home_recv.at[j, a],
                device_id=(t, o, i),
                device_id_type=MESH,
            ).start()

        @pl.when((i == 4) | (i == 7))
        def _():
            slot = jnp.where(i == 4, 4, 1)
            for d in range(8):
                t = lax.rem(h + d, 8)
                border_copy(j, a, t, slot, arrays[a].at[0, :, columns(t, j)]).start()

        @pl.when(relays)
        def _():
            slot = jnp.where(i == 0, 2, 3)
            pltpu.make_async_copy(hop.at[a, j], hop.at[a, j], hop_recv.at[j, a]).wait()
            for d in range(8):
                t = lax.rem(h + d, 8)
                border_copy(j, a, t, slot, hop.at[a, j, t]).start()

    def pass_on(slot, j, a):
        @pl.when(i < 7)
        def _():
            pltpu.make_async_remote_copy(
                src_ref=blk.at[slot, a, j],
                dst_ref=blk.at[slot + 1, a, j],
                send_sem=ring_send,
                recv_sem=ring_recv.at[slot, j, a],
                device_id=(h, o, lax.rem(i + 1, 8)),
                device_id_type=MESH,
            ).start()

    def aux_copy(j, by):
        return pltpu.make_async_remote_copy(
            src_ref=aux.at[0, j],
            dst_ref=aux.at[by, j],
            send_sem=aux_send,
            recv_sem=aux_recv.at[by - 1, j],
            device_id=ahead(by),
            device_id_type=MESH,
        )

    def norms(j):
        query = blk[0, QUERY, j]
        row_max = jnp.full((1, block), -jnp.inf, F32)
        for s in range(WINDOW):
            scores = nt(blk[s, KEY, j], query) * scale2
            weights[s] = scores
            row_max = jnp.maximum(row_max, jnp.max(scores, axis=0, keepdims=True))
        row_sum = jnp.zeros((1, block), F32)
        for s in range(WINDOW):
            e = jnp.exp2(weights[s] - row_max)
            weights[s] = e
            row_sum = row_sum + jnp.sum(e, axis=0, keepdims=True)
        rest = stats_in[j, 0:1, :] * math.log2(math.e)
        offset = stats_in[j, 1:2, :]
        ceiling = jnp.maximum(row_max, rest)
        total = row_sum * jnp.exp2(row_max - ceiling) + jnp.exp2(rest - ceiling)
        log_norm = ceiling + jnp.log2(total)
        row_factor[...] = jnp.exp2(row_max - log_norm)
        for r in range(4):
            lanes = slice(r * 128, (r + 1) * 128)
            aux[0, j, r : r + 1, :] = log_norm[:, lanes]
            aux[0, j, r + 4 : r + 5, :] = offset[:, lanes]
        for by in range(1, WINDOW + 1):
            aux_copy(j, by).start()

    def query_grads(j):
        grad = blk[0, GRAD, j]
        offset = stats_in[j, 1:2, :]
        factor = row_factor[...]
        acc = jnp.zeros((size, block), F32)
        for s in range(WINDOW):
            dweights = nt(blk[s, VALUE, j], grad)
            dscores[...] = ((weights[s] * factor) * (dweights - offset)).astype(BF16)
            acc = acc + tn(blk[s, KEY, j], dscores[...])
        query_out[:, pl.ds(pl.multiple_of(j * size, size), size)] = (acc.T * scale).astype(BF16)

    def key_grads(t, j):
        pltpu.make_async_copy(aux.at[t, j], aux.at[t, j], aux_recv.at[t - 1, j]).wait()
        log_norm = jnp.concatenate([aux[t, j, r : r + 1, :] for r in range(4)], axis=1)
        offset = jnp.concatenate([aux[t, j, r + 4 : r + 5, :] for r in range(4)], axis=1)
        query, grad = blk[t, QUERY, j], blk[t, GRAD, j]
        for part in range(4):
            at = pl.ds(part * 128, 128)
            scores = nt(blk[WINDOW, KEY, j, at, :], query) * scale2
            w = jnp.exp2(scores - log_norm)
            dweights = nt(blk[WINDOW, VALUE, j, at, :], grad)
            ds = (w * (dweights - offset)).astype(BF16)
            key_acc[at, :] += nn(ds, query)
            value_acc[at, :] += nn(w.astype(BF16), grad)

    def clear_accs():
        key_acc[...] = jnp.zeros_like(key_acc)
        value_acc[...] = jnp.zeros_like(value_acc)

    def write_key_grads(j):
        lanes = pl.ds(pl.multiple_of(j * size, size), size)
        key_out[:, lanes] = key_acc[...] * scale
        value_out[:, lanes] = value_acc[...]

    @pl.when(sends_hop)
    def _():
        def one(j, carry):
            send_hops(j)
            return carry

        lax.fori_loop(0, heads, one, 0)

    def first(j, carry):
        for a in range(4):
            send_unit(j, a)
        return carry

    lax.fori_loop(0, LEAD, first, 0)
    pltpu.make_async_copy(blk.at[0, 0, 0:2], blk.at[0, 0, 0:2], own_sem).wait()

    def ticks(jj, carry):
        for a in range(4):

            @pl.when(jj + LEAD < heads)
            def _():
                send_unit(jj + LEAD, a)

            @pl.when(jj < heads)
            def _():
                part = blk.at[0, a, jj, 0 : block - rows, :]
                pltpu.make_async_copy(part, part, home_recv.at[jj, a]).wait()
                pass_on(0, jj, a)

            for s in range(1, WINDOW + 1):
                b = (a - s) % 4
                j = jj if a >= s else jj - 1

                @pl.when((j >= 0) & (j < heads))
                def _():
                    part = blk.at[s, b, j]
                    pltpu.make_async_copy(part, part, ring_recv.at[s - 1, j, b]).wait()
                    if s < WINDOW:
                        pass_on(s, j, b)

            if a == 3:

                @pl.when(jj < heads)
                def _():
                    norms(jj)

            @pl.when(jj >= 1)
            def _():
                j = jj - 1
                if a == 0:
                    query_grads(j)
                elif a == 1:
                    clear_accs()
                    key_grads(1, j)
                    key_grads(2, j)
                elif a == 2:
                    key_grads(3, j)
                else:
                    key_grads(4, j)
                    write_key_grads(j)

        return carry

    lax.fori_loop(0, heads + 1, ticks, 0)

    part = blk.at[0, :, :, 0 : block - rows, :]
    pltpu.make_async_copy(part, part, home_send).wait()
    part = aux.at[1 : WINDOW + 1]
    pltpu.make_async_copy(part, part, aux_send).wait()

    @pl.when(i < 7)
    def _():
        part = blk.at[0:WINDOW]
        pltpu.make_async_copy(part, part, ring_send).wait()

    @pl.when(sends_border)
    def _():
        pltpu.make_async_copy(blk.at[0], blk.at[0], border_send).wait()

    @pl.when(sends_hop)
    def _():
        pltpu.make_async_copy(blk.at[0], blk.at[0], hop_send).wait()


def body(query_states, key_states, value_states, output_grad, saved_offset, rest_mass):
    stats = jnp.stack([rest_mass, saved_offset]).reshape(2, 512, 4).transpose(2, 0, 1)
    any_spec = pl.BlockSpec(memory_space=pl.ANY)
    vmem = pl.BlockSpec(memory_space=pltpu.VMEM)
    dma = pltpu.SemaphoreType.DMA
    outs = pl.pallas_call(
        kernel,
        out_shape=(
            jax.ShapeDtypeStruct((512, 512), BF16),
            jax.ShapeDtypeStruct((512, 512), F32),
            jax.ShapeDtypeStruct((512, 512), F32),
        ),
        in_specs=[any_spec] * 4 + [vmem],
        out_specs=(vmem,) * 3,
        scratch_shapes=[
            pltpu.VMEM((WINDOW + 1, 4, 4, 512, 128), BF16),
            pltpu.VMEM((4, 4, 8, 64, 128), BF16),
            pltpu.VMEM((WINDOW + 1, 4, 8, 128), F32),
            pltpu.VMEM((WINDOW, 512, 512), F32),
            pltpu.VMEM((512, 512), BF16),
            pltpu.VMEM((512, 128), F32),
            pltpu.VMEM((512, 128), F32),
            pltpu.VMEM((1, 512), F32),
            dma,
            dma((4, 4)),
            dma,
            dma,
            dma((WINDOW, 4, 4)),
            dma,
            dma((4, 4)),
            dma,
            dma,
            dma((WINDOW, 4)),
        ],
        compiler_params=pltpu.CompilerParams(
            collective_id=0, has_side_effects=True, vmem_limit_bytes=60 << 20
        ),
        cost_estimate=pl.CostEstimate(
            flops=7_500_000_000, bytes_accessed=5_000_000, transcendentals=8_400_000
        ),
    )(key_states, value_states, query_states, output_grad, stats)
    return tuple(out.reshape(8, 64, 512) for out in outs)


def solution(mesh):
    tokens = P("head", ("outer", "inner"), None)
    heads = P(None, ("outer", "inner"), "head")
    return jax.shard_map(
        body,
        mesh=mesh,
        in_specs=(tokens, tokens, tokens, tokens, heads, heads),
        out_specs=(heads, heads, heads),
        check_vma=False,
    )
```

time: 553 us -> 203 us (0.37)
  the two profiles are of different devices: /device:TPU:24 before, /device:TPU:346 now
where the time goes in v1:
time: 203 us; the launch traced here: 202 us
  Pallas kernels  195 us (96%)
  local copies, waits for them, and re-layouts  6.05 us (3%)
    pallas_call x1, Pallas kernels, body(): pl.pallas_call(kernel, out_shape=(jax.ShapeDtypeStruct((512, 512), BF16),...  195 us
    unnamed x11, local copies, waits for them, and re-layouts  5.89 us

profile of v1, /device:TPU:346, one launch (start us, length us, event | category | flops | bytes accessed | tf_op | source)
XLA Modules:
  0.0 202.2 jit_solution(11375760056983508217)
XLA Ops:
  0.6 0.7 copy.10
  1.4 0.0 copy-start.2
  1.4 0.1 stack.10
  1.4 0.6 copy-done.2
  2.1 0.1 stack.9
  2.2 0.6 maximum_bitcast_fusion.stats_in
  2.8 194.9 %shard_map.85 = (bf16[512,512]{1,0:T(8,128)(2,1)}, f32[512,512]{1,0:T(8,128)}, f32[512,512]{1,0:T(8,128)}) custom-call(bf16[1,64,4096]{2,1,0:T(8,128)(2,1)} %keys.1, bf16[1,64,4096]{2,1,0:T(8,128)(2,1)} %values.1, bf16[1,64,4096]{2,1,0:T(8,128)(2,1)} %queries.1, bf16[1,64,4096]{2,1,0:T(8,128)(2,1)} %grads.1, f32[4,2,512]{2,1,0:T(2,128)} %maximum_bitcast_fusion.stats_in), custom_call_target="tpu_custom_call" | custom-call | flops 7500000256 | bytes 5000000 | tf_op jit(solution)/shard_map/pallas_call | solution.py:321
  197.7 0.0 copy-start.1
  197.7 2.0 copy.14
  199.6 0.0 copy-done.1
  199.6 0.0 copy-start
  199.6 1.0 copy.15
  200.6 0.6 copy-done
  201.2 1.0 copy.16
  (1 shorter events, 0.0 us)
Async XLA Ops:
  1.4 0.7 copy-start.2
  197.7 2.0 copy-start.1
  199.6 1.6 copy-start

commit v2 on v1

v2 whole, which is shorter than its diff:
```python
import functools
import math

import jax
import jax.numpy as jnp
from jax import lax
from jax.experimental import pallas as pl
from jax.experimental.pallas import tpu as pltpu
from jax.sharding import PartitionSpec as P

MESH = pl.DeviceIdType.MESH
F32 = jnp.float32
BF16 = jnp.bfloat16

KEY, QUERY, VALUE, GRAD = range(4)
UNITS = 16
WINDOW = 4
PEER_ORDER = (4, 3, 5, 2, 6, 1, 7)
BORDER_SENDERS = {0: (0, 4), 1: (7, 3)}
LEAD = 2
BORDER_LEAD = 3
HOP_LEAD = BORDER_LEAD + 2


def nt(a, b):
    return lax.dot_general(a, b, (((1,), (1,)), ((), ())), preferred_element_type=F32)


def nn(a, b):
    return lax.dot_general(a, b, (((1,), (0,)), ((), ())), preferred_element_type=F32)


def tn(a, b):
    return lax.dot_general(a, b, (((0,), (0,)), ((), ())), preferred_element_type=F32)


def kernel(
    keys, queries, values, grads, rest_in, offset_in, query_out, key_out, value_out,
    staged, blk, hop, aux, weights, dscores, key_acc, value_acc, row_factor, offsets,
    home_send, home_recv, own_sem, stage_sem, ring_send, ring_recv, hop_send, hop_recv,
    border_send, aux_send, aux_recv,
):
    h, o, i = lax.axis_index("head"), lax.axis_index("outer"), lax.axis_index("inner")
    inputs = (keys, queries, values, grads)
    heads = 4
    rows, size = 64, 128
    block = 8 * rows
    scale = float(size) ** -0.5
    scale2 = scale * math.log2(math.e)
    core = lax.rem(i, 2)
    sibling = i + 1 - 2 * core
    next_o, last_o = lax.rem(o + 1, 8), lax.rem(o + 7, 8)
    my_rows = pl.ds(pl.multiple_of(h * rows, rows), rows)

    def ahead(by):
        at = i + by
        return (h, jnp.where(at > 7, next_o, o), lax.rem(at, 8))

    def behind(by):
        at = i + 8 - by
        return (h, jnp.where(at < 8, last_o, o), lax.rem(at, 8))

    barrier = pltpu.get_barrier_semaphore()

    def greet(device):
        pl.semaphore_signal(barrier, inc=1, device_id=device, device_id_type=MESH)

    for receiver, senders in BORDER_SENDERS.items():

        @pl.when(i == receiver)
        def _():
            for d in range(8):
                for sender in senders:
                    greet((lax.rem(h + d, 8), last_o, sender))

    for d in range(1, 8):
        greet((lax.rem(h + d, 8), o, i))
    for d in range(1, WINDOW + 1):
        greet(behind(d))

    @pl.when(core == 0)
    def _():
        greet((h, o, sibling))

    @pl.when(i == 3)
    def _():
        greet((h, o, 5))

    @pl.when(i == 0)
    def _():
        greet((h, o, 6))

    sends_border = (i == 0) | (i == 3) | (i == 4) | (i == 7)
    sends_hop = (i == 5) | (i == 6)
    relays = (i == 0) | (i == 3)

    def stage(a):
        return pltpu.make_async_copy(inputs[a].at[0], staged.at[a], stage_sem.at[a])

    for a in range(4):
        stage(a).start()

    pl.semaphore_wait(
        barrier, 7 + WINDOW + core + jnp.where(sends_border, 8, 0) + jnp.where(sends_hop, 1, 0)
    )

    for a in range(4):
        stage(a).wait()

    for a in range(4):
        for j in range(heads):
            pltpu.make_async_copy(
                staged.at[a, :, pl.ds(pl.multiple_of(h * 512 + j * size, size), size)],
                blk.at[0, a, j, my_rows, :],
                own_sem,
            ).start()

    def columns(t, j):
        return pl.ds(pl.multiple_of(t * 512 + j * size, size), size)

    def hop_copy(j, a, t):
        return pltpu.make_async_remote_copy(
            src_ref=staged.at[a, :, columns(t, j)],
            dst_ref=hop.at[a, j, t],
            send_sem=hop_send,
            recv_sem=hop_recv.at[j, a],
            device_id=(h, o, jnp.where(i == 5, 3, 0)),
            device_id_type=MESH,
        )

    def border_copy(j, a, t, slot, source):
        return pltpu.make_async_remote_copy(
            src_ref=source,
            dst_ref=blk.at[slot, a, j, my_rows, :],
            send_sem=border_send,
            recv_sem=ring_recv.at[slot - 1, j, a],
            device_id=(t, next_o, jnp.where((i == 3) | (i == 7), 1, 0)),
            device_id_type=MESH,
        )

    def send_hops(j, a):
        @pl.when(sends_hop)
        def _():
            for t in range(8):
                hop_copy(j, a, t).start()

    def send_unit(j, a):
        for d in PEER_ORDER:
            t = lax.rem(h + d, 8)
            pltpu.make_async_remote_copy(
                src_ref=staged.at[a, :, columns(t, j)],
                dst_ref=blk.at[0, a, j, my_rows, :],
                send_sem=home_send,
                recv_sem=home_recv.at[j, a],
                device_id=(t, o, i),
                device_id_type=MESH,
            ).start()

    def send_border(j, a):
        @pl.when((i == 4) | (i == 7))
        def _():
            slot = jnp.where(i == 4, 4, 2)
            for d in range(8):
                t = lax.rem(h + d, 8)
                border_copy(j, a, t, slot, staged.at[a, :, columns(t, j)]).start()

        @pl.when(relays)
        def _():
            slot = jnp.where(i == 0, 2, 4)
            pltpu.make_async_copy(hop.at[a, j], hop.at[a, j], hop_recv.at[j, a]).wait()
            for d in range(8):
                t = lax.rem(h + d, 8)
                border_copy(j, a, t, slot, hop.at[a, j, t]).start()

    def pass_on(slot, to_slot, to, j, a):
        pltpu.make_async_remote_copy(
            src_ref=blk.at[slot, a, j],
            dst_ref=blk.at[to_slot, a, j],
            send_sem=ring_send,
            recv_sem=ring_recv.at[to_slot - 1, j, a],
            device_id=(h, o, to),
            device_id_type=MESH,
        ).start()

    def to_next_chip(slot, j, a):
        @pl.when(i < 6)
        def _():
            pass_on(slot, slot + 2, lax.rem(i + 2, 8), j, a)

    def to_sibling(slot, to_slot, from_core, j, a):
        @pl.when(core == from_core)
        def _():
            pass_on(slot, to_slot, sibling, j, a)

    def await_slot(s, j, a):
        part = blk.at[s, a, j]
        pltpu.make_async_copy(part, part, ring_recv.at[s - 1, j, a]).wait()

    def aux_copy(j, by):
        return pltpu.make_async_remote_copy(
            src_ref=aux.at[0, j],
            dst_ref=aux.at[by, j],
            send_sem=aux_send,
            recv_sem=aux_recv.at[by - 1, j],
            device_id=ahead(by),
            device_id_type=MESH,
        )

    def row_of(ref, j):
        return jnp.concatenate([ref[a, pl.ds(j, 1), :] for a in range(8)], axis=1)

    def norms(j):
        query = blk[0, QUERY, j]
        row_max = jnp.full((1, block), -jnp.inf, F32)
        for s in range(WINDOW):
            scores = nt(blk[s, KEY, j], query) * scale2
            weights[j, s] = scores
            row_max = jnp.maximum(row_max, jnp.max(scores, axis=0, keepdims=True))
        row_sum = jnp.zeros((1, block), F32)
        for s in range(WINDOW):
            e = jnp.exp2(weights[j, s] - row_max)
            weights[j, s] = e
            row_sum = row_sum + jnp.sum(e, axis=0, keepdims=True)
        rest = row_of(rest_in, j) * math.log2(math.e)
        offset = row_of(offset_in, j)
        offsets[j] = offset
        ceiling = jnp.maximum(row_max, rest)
        total = row_sum * jnp.exp2(row_max - ceiling) + jnp.exp2(rest - ceiling)
        log_norm = ceiling + jnp.log2(total)
        row_factor[j] = jnp.exp2(row_max - log_norm)
        for r in range(4):
            lanes = slice(r * 128, (r + 1) * 128)
            aux[0, j, r : r + 1, :] = log_norm[:, lanes]
            aux[0, j, r + 4 : r + 5, :] = offset[:, lanes]
        for by in range(1, WINDOW + 1):
            aux_copy(j, by).start()

    def query_grads(j):
        grad = blk[0, GRAD, j]
        offset = offsets[j]
        factor = row_factor[j]
        acc = jnp.zeros((size, block), F32)
        for s in range(WINDOW):
            dweights = nt(blk[s, VALUE, j], grad)
            dscores[...] = ((weights[j, s] * factor) * (dweights - offset)).astype(BF16)
            acc = acc + tn(blk[s, KEY, j], dscores[...])
        query_out[:, pl.ds(pl.multiple_of(j * size, size), size)] = (acc.T * scale).astype(BF16)

    def key_grads(t, j):
        pltpu.make_async_copy(aux.at[t, j], aux.at[t, j], aux_recv.at[t - 1, j]).wait()
        log_norm = jnp.concatenate([aux[t, j, r : r + 1, :] for r in range(4)], axis=1)
        offset = jnp.concatenate([aux[t, j, r + 4 : r + 5, :] for r in range(4)], axis=1)
        query, grad = blk[t, QUERY, j], blk[t, GRAD, j]
        for part in range(4):
            at = pl.ds(part * 128, 128)
            scores = nt(blk[WINDOW, KEY, j, at, :], query) * scale2
            w = jnp.exp2(scores - log_norm)
            dweights = nt(blk[WINDOW, VALUE, j, at, :], grad)
            ds = (w * (dweights - offset)).astype(BF16)
            key_acc[at, :] += nn(ds, query)
            value_acc[at, :] += nn(w.astype(BF16), grad)

    def clear_accs():
        key_acc[...] = jnp.zeros_like(key_acc)
        value_acc[...] = jnp.zeros_like(value_acc)

    def write_key_grads(j):
        lanes = pl.ds(pl.multiple_of(j * size, size), size)
        key_out[:, lanes] = key_acc[...] * scale
        value_out[:, lanes] = value_acc[...]

    def unit(u, do):
        @pl.when((u >= 0) & (u < UNITS))
        def _():
            do(lax.rem(u, 8) // 2, 2 * (u // 8) + lax.rem(u, 2))

    def from_u(start, do):
        def one(u, carry):
            unit(u, do)
            return carry

        lax.fori_loop(0, start, one, 0)

    def home(j, b):
        part = blk.at[0, b, j, 0 : block - rows, :]
        pltpu.make_async_copy(part, part, home_recv.at[j, b]).wait()
        to_next_chip(0, j, b)
        to_sibling(0, 1, 0, j, b)

    def near(j, b):
        await_slot(2, j, b)
        to_next_chip(2, j, b)
        to_sibling(2, 3, 0, j, b)
        to_sibling(2, 1, 1, j, b)

    def far(j, b):
        await_slot(4, j, b)
        to_sibling(4, 3, 1, j, b)

    from_u(HOP_LEAD, send_hops)
    from_u(LEAD, send_unit)
    from_u(BORDER_LEAD, send_border)
    pltpu.make_async_copy(blk.at[0, 0, 0:2], blk.at[0, 0, 0:2], own_sem).wait()

    def ticks(tick, carry):
        unit(tick, home)
        unit(tick - 1, near)
        unit(tick - 2, far)
        unit(tick + HOP_LEAD, send_hops)
        unit(tick + LEAD, send_unit)
        unit(tick + BORDER_LEAD, send_border)
        unit(tick - 2, functools.partial(await_slot, 1))
        unit(tick - 3, functools.partial(await_slot, 3))

        def at_turn(by, do):
            j = (tick - by) // 2

            @pl.when((lax.rem(tick + 64 - by, 2) == 0) & (j >= 0) & (j < heads))
            def _():
                do(j)

        def first_keys(j):
            clear_accs()
            key_grads(2, j)

        def more_keys(j):
            query_grads(j)
            key_grads(1, j)
            key_grads(4, j)

        def last_keys(j):
            key_grads(3, j)
            write_key_grads(j)

        at_turn(3, norms)
        at_turn(12, last_keys)
        at_turn(10, first_keys)
        at_turn(11, more_keys)
        return carry

    lax.fori_loop(0, UNITS + 3, ticks, 0)

    part = blk.at[0, :, :, 0 : block - rows, :]
    pltpu.make_async_copy(part, part, home_send).wait()
    part = aux.at[1 : WINDOW + 1]
    pltpu.make_async_copy(part, part, aux_send).wait()

    part = blk.at[0:2]
    pltpu.make_async_copy(part, part, ring_send).wait()

    @pl.when(i < 6)
    def _():
        pltpu.make_async_copy(part, part, ring_send).wait()

    @pl.when(sends_border)
    def _():
        pltpu.make_async_copy(blk.at[0], blk.at[0], border_send).wait()

    @pl.when(sends_hop)
    def _():
        pltpu.make_async_copy(blk.at[0], blk.at[0], hop_send).wait()


def body(query_states, key_states, value_states, output_grad, saved_offset, rest_mass):
    rest, offset = rest_mass.transpose(0, 2, 1), saved_offset.transpose(0, 2, 1)
    any_spec = pl.BlockSpec(memory_space=pl.ANY)
    vmem = pl.BlockSpec(memory_space=pltpu.VMEM)
    dma = pltpu.SemaphoreType.DMA
    outs = pl.pallas_call(
        kernel,
        out_shape=(
            pltpu.VMEM((512, 512), BF16),
            pltpu.VMEM((512, 512), F32),
            pltpu.VMEM((512, 512), F32),
        ),
        in_specs=[any_spec] * 4 + [vmem] * 2,
        out_specs=(vmem,) * 3,
        scratch_shapes=[
            pltpu.VMEM((4, 64, 4096), BF16),
            pltpu.VMEM((WINDOW + 1, 4, 4, 512, 128), BF16),
            pltpu.VMEM((4, 4, 8, 64, 128), BF16),
            pltpu.VMEM((WINDOW + 1, 4, 8, 128), F32),
            pltpu.VMEM((4, WINDOW, 512, 512), F32),
            pltpu.VMEM((512, 512), BF16),
            pltpu.VMEM((512, 128), F32),
            pltpu.VMEM((512, 128), F32),
            pltpu.VMEM((4, 1, 512), F32),
            pltpu.VMEM((4, 1, 512), F32),
            dma,
            dma((4, 4)),
            dma,
            dma((4,)),
            dma,
            dma((WINDOW, 4, 4)),
            dma,
            dma((4, 4)),
            dma,
            dma,
            dma((WINDOW, 4)),
        ],
        compiler_params=pltpu.CompilerParams(
            collective_id=0, has_side_effects=True, vmem_limit_bytes=60 << 20
        ),
        cost_estimate=pl.CostEstimate(
            flops=7_500_000_000, bytes_accessed=5_000_000, transcendentals=8_400_000
        ),
    )(key_states, query_states, value_states, output_grad, rest, offset)
    return tuple(out.reshape(8, 64, 512) for out in outs)


def solution(mesh):
    tokens = P("head", ("outer", "inner"), None)
    heads = P(None, ("outer", "inner"), "head")
    return jax.shard_map(
        body,
        mesh=mesh,
        in_specs=(tokens, tokens, tokens, tokens, heads, heads),
        out_specs=(heads, heads, heads),
        check_vma=False,
    )
```

time: 203 us -> 182 us (0.90)
  the two profiles are of different devices: /device:TPU:346 before, /device:TPU:14 now
where the time goes in v2:
time: 182 us
  Pallas kernels  179 us (98%)
  local copies, waits for them, and re-layouts  2.73 us (2%)
    pallas_call x1, Pallas kernels, body(): pl.pallas_call(kernel, out_shape=(pltpu.VMEM((512, 512), BF16), pltpu.VME...  179 us

profile of v2, /device:TPU:14, one launch (start us, length us, event | category | flops | bytes accessed | tf_op | source)
XLA Modules:
  0.0 182.0 jit_solution(4986595532292686944)
XLA Ops:
  0.6 178.6 %shard_map.85 = (bf16[512,512]{1,0:T(8,128)(2,1)S(1)}, f32[512,512]{1,0:T(8,128)S(1)}, f32[512,512]{1,0:T(8,128)S(1)}) custom-call(bf16[1,64,4096]{2,1,0:T(8,128)(2,1)} %keys.1, bf16[1,64,4096]{2,1,0:T(8,128)(2,1)} %queries.1, bf16[1,64,4096]{2,1,0:T(8,128)(2,1)} %values.1, bf16[1,64,4096]{2,1,0:T(8,128)(2,1)} %grads.1, f32[8,4,64]{2,1,0:T(4,128)} %bitcast.8, ...), custom_call_target="tpu_custom_call" | custom-call | flops 7500000256 | bytes 5000000 | tf_op jit(solution)/shard_map/pallas_call | solution.py:369
  179.2 0.8 copy.12
  180.0 1.0 copy.13
  181.0 1.0 copy.14

commit v3 on v2

--- a/solution.py
+++ b/solution.py
@@ -17,9 +17,9 @@
 WINDOW = 4
 PEER_ORDER = (4, 3, 5, 2, 6, 1, 7)
 BORDER_SENDERS = {0: (0, 4), 1: (7, 3)}
-LEAD = 2
-BORDER_LEAD = 3
-HOP_LEAD = BORDER_LEAD + 2
+LEADS = ((5, 4), (9, 3), (UNITS, 2))
+BORDER_MORE = 1
+HOP_MORE = BORDER_MORE + 2
 
 
 def nt(a, b):
@@ -251,14 +251,12 @@
         log_norm = jnp.concatenate([aux[t, j, r : r + 1, :] for r in range(4)], axis=1)
         offset = jnp.concatenate([aux[t, j, r + 4 : r + 5, :] for r in range(4)], axis=1)
         query, grad = blk[t, QUERY, j], blk[t, GRAD, j]
-        for part in range(4):
-            at = pl.ds(part * 128, 128)
-            scores = nt(blk[WINDOW, KEY, j, at, :], query) * scale2
-            w = jnp.exp2(scores - log_norm)
-            dweights = nt(blk[WINDOW, VALUE, j, at, :], grad)
-            ds = (w * (dweights - offset)).astype(BF16)
-            key_acc[at, :] += nn(ds, query)
-            value_acc[at, :] += nn(w.astype(BF16), grad)
+        scores = nt(blk[WINDOW, KEY, j], query) * scale2
+        w = jnp.exp2(scores - log_norm)
+        dweights = nt(blk[WINDOW, VALUE, j], grad)
+        ds = (w * (dweights - offset)).astype(BF16)
+        key_acc[...] += nn(ds, query)
+        value_acc[...] += nn(w.astype(BF16), grad)
 
     def clear_accs():
         key_acc[...] = jnp.zeros_like(key_acc)
@@ -297,18 +295,25 @@
         await_slot(4, j, b)
         to_sibling(4, 3, 1, j, b)
 
-    from_u(HOP_LEAD, send_hops)
-    from_u(LEAD, send_unit)
-    from_u(BORDER_LEAD, send_border)
+    from_u(LEADS[0][1] + HOP_MORE, send_hops)
+    from_u(LEADS[0][1], send_unit)
+    from_u(LEADS[0][1] + BORDER_MORE, send_border)
     pltpu.make_async_copy(blk.at[0, 0, 0:2], blk.at[0, 0, 0:2], own_sem).wait()
 
     def ticks(tick, carry):
         unit(tick, home)
         unit(tick - 1, near)
         unit(tick - 2, far)
-        unit(tick + HOP_LEAD, send_hops)
-        unit(tick + LEAD, send_unit)
-        unit(tick + BORDER_LEAD, send_border)
+        first = 0
+        for last, lead in LEADS:
+
+            @pl.when((tick >= first) & (tick <= last))
+            def _():
+                unit(tick + lead + HOP_MORE, send_hops)
+                unit(tick + lead, send_unit)
+                unit(tick + lead + BORDER_MORE, send_border)
+
+            first = last + 2
         unit(tick - 2, functools.partial(await_slot, 1))
         unit(tick - 3, functools.partial(await_slot, 3))
 

time: 182 us -> 174 us (0.956)
  the two profiles are of different devices: /device:TPU:14 before, /device:TPU:6 now
where the time goes in v3:
time: 174 us
  Pallas kernels  171 us (98%)
  local copies, waits for them, and re-layouts  2.73 us (2%)
    pallas_call x1, Pallas kernels, body(): pl.pallas_call(kernel, out_shape=(pltpu.VMEM((512, 512), BF16), pltpu.VME...  171 us

profile of v3, /device:TPU:6, one launch (start us, length us, event | category | flops | bytes accessed | tf_op | source)
XLA Modules:
  0.0 173.9 jit_solution(1928434871992822165)
XLA Ops:
  0.6 170.5 %shard_map.85 = (bf16[512,512]{1,0:T(8,128)(2,1)S(1)}, f32[512,512]{1,0:T(8,128)S(1)}, f32[512,512]{1,0:T(8,128)S(1)}) custom-call(bf16[1,64,4096]{2,1,0:T(8,128)(2,1)} %keys.1, bf16[1,64,4096]{2,1,0:T(8,128)(2,1)} %queries.1, bf16[1,64,4096]{2,1,0:T(8,128)(2,1)} %values.1, bf16[1,64,4096]{2,1,0:T(8,128)(2,1)} %grads.1, f32[8,4,64]{2,1,0:T(4,128)} %bitcast.8, ...), custom_call_target="tpu_custom_call" | custom-call | flops 7500000256 | bytes 5000000 | tf_op jit(solution)/shard_map/pallas_call | solution.py:374
  171.2 0.8 copy.12
  171.9 1.0 copy.13
  172.9 1.0 copy.14

commit v4 on v3

--- a/solution.py
+++ b/solution.py
@@ -14,6 +14,7 @@
 
 KEY, QUERY, VALUE, GRAD = range(4)
 UNITS = 16
+DIRECT_FROM = 14
 WINDOW = 4
 PEER_ORDER = (4, 3, 5, 2, 6, 1, 7)
 BORDER_SENDERS = {0: (0, 4), 1: (7, 3)}
@@ -37,7 +38,7 @@
 def kernel(
     keys, queries, values, grads, rest_in, offset_in, query_out, key_out, value_out,
     staged, blk, hop, aux, weights, dscores, key_acc, value_acc, row_factor, offsets,
-    home_send, home_recv, own_sem, stage_sem, ring_send, ring_recv, hop_send, hop_recv,
+    home_send, home_recv, direct_send, own_sem, stage_sem, ring_send, ring_recv, hop_send, hop_recv,
     border_send, aux_send, aux_recv,
 ):
     h, o, i = lax.axis_index("head"), lax.axis_index("outer"), lax.axis_index("inner")
@@ -172,11 +173,11 @@
                 t = lax.rem(h + d, 8)
                 border_copy(j, a, t, slot, hop.at[a, j, t]).start()
 
-    def pass_on(slot, to_slot, to, j, a):
+    def pass_on(slot, to_slot, to, j, a, sent=ring_send):
         pltpu.make_async_remote_copy(
             src_ref=blk.at[slot, a, j],
             dst_ref=blk.at[to_slot, a, j],
-            send_sem=ring_send,
+            send_sem=sent,
             recv_sem=ring_recv.at[to_slot - 1, j, a],
             device_id=(h, o, to),
             device_id_type=MESH,
@@ -279,15 +280,27 @@
 
         lax.fori_loop(0, start, one, 0)
 
+    def is_late(j, b):
+        return 8 * (b // 2) + 2 * j + lax.rem(b, 2) >= DIRECT_FROM
+
     def home(j, b):
         part = blk.at[0, b, j, 0 : block - rows, :]
         pltpu.make_async_copy(part, part, home_recv.at[j, b]).wait()
         to_next_chip(0, j, b)
+
+        @pl.when(is_late(j, b) & (i < 4))
+        def _():
+            pass_on(0, 4, lax.rem(i + 4, 8), j, b, direct_send)
+
         to_sibling(0, 1, 0, j, b)
 
     def near(j, b):
         await_slot(2, j, b)
-        to_next_chip(2, j, b)
+
+        @pl.when((i < 2) | jnp.logical_not(is_late(j, b)))
+        def _():
+            to_next_chip(2, j, b)
+
         to_sibling(2, 3, 0, j, b)
         to_sibling(2, 1, 1, j, b)
 
@@ -353,9 +366,28 @@
     part = blk.at[0:2]
     pltpu.make_async_copy(part, part, ring_send).wait()
 
+    whole = blk.at[0]
+
     @pl.when(i < 6)
     def _():
-        pltpu.make_async_copy(part, part, ring_send).wait()
+        pltpu.make_async_copy(whole, whole, ring_send).wait()
+
+    @pl.when(i < 2)
+    def _():
+        pltpu.make_async_copy(whole, whole, ring_send).wait()
+
+    late = UNITS - DIRECT_FROM
+
+    @pl.when((i >= 2) & (i < 6))
+    def _():
+        for units in (8, DIRECT_FROM - 8):
+            part = blk.at[0:units, 0, 0] if units <= WINDOW else blk.at[0 : units // 2, 0, 0:2]
+            pltpu.make_async_copy(part, part, ring_send).wait()
+
+    @pl.when(i < 4)
+    def _():
+        part = blk.at[0:late, 0, 0]
+        pltpu.make_async_copy(part, part, direct_send).wait()
 
     @pl.when(sends_border)
     def _():
@@ -394,6 +426,7 @@
             dma,
             dma((4, 4)),
             dma,
+            dma,
             dma((4,)),
             dma,
             dma((WINDOW, 4, 4)),

time: 174 us -> 174 us (level)
  Pallas kernels: 171 us -> 169 us
where the time goes in v4:
time: 174 us; the launch traced here: 173 us
  Pallas kernels  169 us (97%)
  local copies, waits for them, and re-layouts  2.73 us (2%)
    pallas_call x1, Pallas kernels, body(): pl.pallas_call(kernel, out_shape=(pltpu.VMEM((512, 512), BF16), pltpu.VME...  169 us

profile of v4, /device:TPU:6, one launch (start us, length us, event | category | flops | bytes accessed | tf_op | source)
XLA Modules:
  0.0 172.8 jit_solution(11529727250368901510)
XLA Ops:
  0.6 169.5 %shard_map.85 = (bf16[512,512]{1,0:T(8,128)(2,1)S(1)}, f32[512,512]{1,0:T(8,128)S(1)}, f32[512,512]{1,0:T(8,128)S(1)}) custom-call(bf16[1,64,4096]{2,1,0:T(8,128)(2,1)} %keys.1, bf16[1,64,4096]{2,1,0:T(8,128)(2,1)} %queries.1, bf16[1,64,4096]{2,1,0:T(8,128)(2,1)} %values.1, bf16[1,64,4096]{2,1,0:T(8,128)(2,1)} %grads.1, f32[8,4,64]{2,1,0:T(4,128)} %bitcast.8, ...), custom_call_target="tpu_custom_call" | custom-call | flops 7500000256 | bytes 5000000 | tf_op jit(solution)/shard_map/pallas_call | solution.py:406
  170.1 0.8 copy.12
  170.9 1.0 copy.13
  171.9 1.0 copy.14
